TPU v7x, 256 devices: a whole 4x4x8 slice. The times are simulated.
256 devices in a mesh: ctx: 32 (over y, x, core), tp: 4 (over z_hi), dp: 2 (over z_lo).
Axes of the slice: x: 4, y: 4, z: 8 (z_hi: 4, z_lo: 2; z = z_hi * 2 + z_lo), core: 2. Of those that a mesh axis runs over, the one named last changes fastest.
Arguments:
- residual: bfloat16 [2, 4096, 2048], P('dp', 'ctx', 'tp'), may hold values from -3 to 3
- queries: bfloat16 [2, 4096, 2048], P('dp', 'ctx', 'tp'), may hold values from -6 to 6
- attn_keys: bfloat16 [2, 4096, 2048], P('dp', 'ctx', 'tp'), may hold values from -6 to 6
- attn_values: bfloat16 [2, 4096, 2048], P('dp', 'ctx', 'tp'), may hold values from -24 to 24
- gate_table: bfloat16 [1000, 2048], P(None, 'tp'), may hold values from 0.19921875 to 1.796875
- timesteps: int32 [2], P('dp'), may hold values from 0 to 999
- enc_feats: bfloat16 [2, 1536, 1536], P('dp', 'ctx', 'tp'), may hold values from -6 to 6
- tap_rows: int32 [2, 4096, 4], P('dp', 'ctx'), may hold values from 0 to 1535
- tap_weights: float32 [2, 4096, 4], P('dp', 'ctx'), may hold values from 0.1 to 1
- proj_in: bfloat16 [2048, 2048], P('tp'), may hold values from -0.125 to 0.125
- proj_out: bfloat16 [2048, 1536], P('tp'), may hold values from -0.125 to 0.125
Outputs:
- d_hidden: bfloat16 [2, 4096, 2048], P('dp', 'ctx', 'tp')
- grad_proj_in: float32 [2048, 2048], P('tp', 'ctx')
- grad_proj_out: float32 [2048, 1536], P('tp', 'ctx')
All inputs are finite; a program needn't handle non-finite values.
Results may differ from a plain program's by a relative error of at most 0.025.
Values may be sent and summed in bfloat16 or wider, within the bound.
A program may use at most 64 MiB of HBM per device.

v0:
```python
import jax
import jax.numpy as jnp
from jax import lax
from jax.sharding import PartitionSpec as P

HD = 128


eps = 1e-06
loss_scale = 4194304.0


def silu_slope(inner):
    sigma = jax.nn.sigmoid(inner)
    return sigma * (1.0 + inner * (1.0 - sigma))


def local(
    residual,
    queries,
    attn_keys,
    attn_values,
    gate_table,
    timesteps,
    enc_feats,
    tap_rows,
    tap_weights,
    proj_in,
    proj_out,
):
    token_count = queries.shape[1]
    local_width = queries.shape[2]
    head_count = local_width // HD
    query_heads = queries[0].reshape(token_count, head_count, HD)

    def key_block(state, blocks):
        old_max, running_sum, weighted = state
        key_piece = blocks[0].reshape(-1, head_count, HD)
        value_piece = blocks[1].reshape(-1, head_count, HD)
        scores = jnp.einsum(
            "qhd,khd->hqk", query_heads, key_piece, preferred_element_type=jnp.float32
        ) * HD ** (-0.5)
        new_max = jnp.maximum(old_max, jnp.max(scores, axis=2))
        expo = jnp.exp(scores - new_max[:, :, None])
        shrink = jnp.exp(old_max - new_max)
        running_sum = running_sum * shrink + jnp.sum(expo, axis=2)
        update = jnp.einsum(
            "hqk,khd->hqd",
            expo.astype(jnp.bfloat16),
            value_piece,
            preferred_element_type=jnp.float32,
        )
        weighted = weighted * shrink[:, :, None] + update
        return ((new_max, running_sum, weighted), None)

    start_state = (
        jnp.full((head_count, token_count), -1e30, jnp.float32),
        jnp.zeros((head_count, token_count), jnp.float32),
        jnp.zeros((head_count, token_count, HD), jnp.float32),
    )
    carry = start_state
    pieces = (
        lax.all_gather(attn_keys[0], "ctx", axis=0, tiled=True),
        lax.all_gather(attn_values[0], "ctx", axis=0, tiled=True),
    )
    row_total = pieces[0].shape[0]
    block_rows = 512
    block_count = row_total // block_rows
    key_blocks = pieces[0].reshape(block_count, block_rows, pieces[0].shape[1])
    value_blocks = pieces[1].reshape(block_count, block_rows, pieces[1].shape[1])
    carry, unused = lax.scan(key_block, carry, (key_blocks, value_blocks))
    final_max, running_sum, weighted = carry
    attention = (
        (weighted / running_sum[:, :, None]).transpose(1, 0, 2).reshape(token_count, local_width)
    )
    selector = (jnp.arange(gate_table.shape[0]) == timesteps[0]).astype(jnp.bfloat16)[None, :]
    gate_row = jnp.dot(selector, gate_table, preferred_element_type=jnp.float32)
    hidden = (residual[0].astype(jnp.float32) + gate_row * attention).astype(jnp.bfloat16)
    slab = proj_in
    inner_t = lax.psum_scatter(
        lax.dot_general(
            slab, hidden, (((0,), (1,)), ((), ())), preferred_element_type=jnp.float32
        ).astype(jnp.bfloat16),
        "tp",
        scatter_dimension=0,
        tiled=True,
    ).astype(jnp.float32)
    activation_t = jax.nn.silu(inner_t).astype(jnp.bfloat16)
    slab = proj_out
    projected_t = lax.psum_scatter(
        lax.dot_general(
            slab, activation_t, (((0,), (0,)), ((), ())), preferred_element_type=jnp.float32
        ).astype(jnp.bfloat16),
        "tp",
        scatter_dimension=0,
        tiled=True,
    ).astype(jnp.float32)
    encoder_all = lax.all_gather(enc_feats[0], "ctx", axis=0, tiled=True)
    picked = jnp.take(encoder_all, tap_rows[0], axis=0).astype(jnp.float32)
    tap_norm = tap_weights[0] / jnp.sum(tap_weights[0], axis=1, keepdims=True)
    target_t = jnp.einsum("rk,rkc->cr", tap_norm, picked)
    square_p, square_t, product = lax.psum(
        (
            jnp.sum(projected_t * projected_t, axis=0),
            jnp.sum(target_t * target_t, axis=0),
            jnp.sum(projected_t * target_t, axis=0),
        ),
        "tp",
    )
    norm_p = jnp.sqrt(square_p + eps)
    norm_t = jnp.sqrt(square_t + eps)
    cosine = product / (norm_p * norm_t)
    all_tokens = token_count * lax.axis_size("ctx") * queries.shape[0] * lax.axis_size("dp")
    factor = loss_scale / all_tokens
    grad_proj_t = (
        -factor * (target_t / (norm_p * norm_t) - cosine * projected_t / (norm_p * norm_p))
    ).astype(jnp.bfloat16)
    grad_full = lax.all_gather(grad_proj_t, "tp", axis=0, tiled=True)
    grad_act_t = jnp.dot(proj_out, grad_full, preferred_element_type=jnp.float32)
    grad_inner_t = (grad_act_t * silu_slope(inner_t)).astype(jnp.bfloat16)
    inner_full = lax.all_gather(grad_inner_t, "tp", axis=0, tiled=True)
    hidden_grad_t = jnp.dot(proj_in, inner_full, preferred_element_type=jnp.float32)
    d_hidden = hidden_grad_t.T.astype(jnp.bfloat16)[None]
    slab = inner_full
    inner_piece = lax.psum_scatter(
        jnp.dot(slab, hidden, preferred_element_type=jnp.float32).astype(jnp.bfloat16),
        "ctx",
        scatter_dimension=0,
        tiled=True,
    )
    slab = grad_full
    outer_piece = lax.psum_scatter(
        lax.dot_general(
            slab, activation_t, (((1,), (1,)), ((), ())), preferred_element_type=jnp.float32
        ).astype(jnp.bfloat16),
        "ctx",
        scatter_dimension=0,
        tiled=True,
    )
    inner_sum, outer_sum = (
        lax.psum(inner_piece, "dp").astype(jnp.float32),
        lax.psum(outer_piece, "dp").astype(jnp.float32),
    )
    return (d_hidden, inner_sum.T, outer_sum.T)


def solution(mesh):
    in_specs = (
        P("dp", "ctx", "tp"),
        P("dp", "ctx", "tp"),
        P("dp", "ctx", "tp"),
        P("dp", "ctx", "tp"),
        P(None, "tp"),
        P("dp"),
        P("dp", "ctx", "tp"),
        P("dp", "ctx", None),
        P("dp", "ctx", None),
        P("tp", None),
        P("tp", None),
    )
    out_specs = (P("dp", "ctx", "tp"), P("tp", "ctx"), P("tp", "ctx"))
    return jax.shard_map(local, mesh=mesh, in_specs=in_specs, out_specs=out_specs, check_vma=False)
```

profile of v0, /device:TPU:10, one launch (start us, length us, event | category | flops | bytes accessed | tf_op | source)
XLA Modules:
  0.0 558.1 jit_solution(8063370601680744958)
XLA Ops:
  14.3 48.7 %all-gather.9.cloned.1.call-done = bf16[1,4096,512]{2,1,0:T(8,128)(2,1)} async-done(((bf16[1,128,512]{2,1,0:T(8,128)(2,1)}), bf16[1,4096,512]{2,1,0:T(8,128)(2,1)}) %all-gather.9.cloned.1.call-update) | async-done | bytes 4194320 | tf_op jit(solution)/shard_map/all_gather | solution.py:63
  63.0 53.1 %all-gather.11.cloned.1.call-done = bf16[1,4096,512]{2,1,0:T(8,128)(2,1)} async-done(((bf16[1,128,512]{2,1,0:T(8,128)(2,1)}), bf16[1,4096,512]{2,1,0:T(8,128)(2,1)}) %all-gather.11.cloned.1.call-update) | async-done | bytes 4194320 | tf_op jit(solution)/shard_map/all_gather | solution.py:64
  116.1 67.2 %while.15 = (s32[]{:T(128)}, f32[4,128]{1,0:T(4,128)S(1)}, f32[4,128]{1,0:T(4,128)S(1)}, f32[4,128,128]{2,1,0:T(8,128)S(1)}, bf16[8,512,512]{2,1,0:T(8,128)(2,1)...) while((s32[]{:T(128)}, f32[4,128]{1,0:T(4,128)S(1)}, ...), condition=%wide.region_4.5_spmd.clone, body=%wide.region_1.4_spmd.clone.sunk | while | flops 135989760 | bytes 9076845 | solution.py:71
  120.9 2.1 copy.62
  129.3 2.1 copy.62
  132.9 2.1 constant_dynamic-slice_fusion.3
  137.7 2.1 copy.62
  146.1 2.1 copy.62
  149.7 2.1 constant_dynamic-slice_fusion.3
  154.5 2.1 copy.62
  162.9 2.1 copy.62
  171.3 2.1 copy.62
  179.7 2.1 copy.62
  186.8 27.5 %reduce-scatter.7.cloned.1.call-done = bf16[512,128]{0,1:T(8,128)(2,1)} async-done(((bf16[2048,128]{0,1:T(8,128)(2,1)}), bf16[512,128]{0,1:T(8,128)(2,1)}) %reduce-scatter.7.cloned.1.call-update) | async-done | bytes 131088 | tf_op jit(solution)/shard_map/reduce_scatter | solution.py:80
  217.5 44.6 %all-gather.7.cloned.1.call-done = bf16[1,1536,384]{2,1,0:T(8,128)(2,1)} async-done(((bf16[1,48,384]{2,1,0:T(8,128)(2,1)}), bf16[1,1536,384]{2,1,0:T(8,128)(2,1)}) %all-gather.7.cloned.1.call-update) | async-done | bytes 1179664 | tf_op jit(solution)/shard_map/all_gather | solution.py:98
  262.1 3.2 gather_fusion
  266.0 26.3 %reduce-scatter.13.cloned.1.call-done = bf16[384,128]{1,0:T(8,128)(2,1)} async-done(((bf16[1536,128]{1,0:T(8,128)(2,1)}), bf16[384,128]{1,0:T(8,128)(2,1)}) %reduce-scatter.13.cloned.1.call-update) | async-done | bytes 98320
  293.4 10.9 %all-reduce = (f32[128]{0:T(128)S(1)}, f32[128]{0:T(128)S(1)}, f32[128]{0:T(128)S(1)}) all-reduce(f32[128]{0:T(128)S(1)} %get-tuple-element.90, f32[128]{0:T(128)S(1)} %get-tuple-element.89, f32[128]{0:T(128)S(1)} %get-tuple-element.88), channel_id=1, replica_groups=mesh['ctx'=32,'tp'=4,'dp'=2] {'tp'}, use_global_device_ids=true, to_apply=%region_8.9 | all-reduce | flops 384 | bytes 3072 | tf_op jit(solution)/shard_map/psum | solution.py:102
  304.5 15.5 %all_gather.18 = bf16[1536,128]{0,1:T(8,128)(2,1)S(1)} all-gather(bf16[384,128]{0,1:T(8,128)(2,1)S(1)} %fusion.29), channel_id=1, replica_groups=mesh['ctx'=32,'tp'=4,'dp'=2] {'tp'}, dimensions={0}, use_global_device_ids=true | all-gather | bytes 491520 | tf_op jit(solution)/shard_map/all_gather | solution.py:118
  322.1 16.0 %all_gather.19 = bf16[2048,128]{0,1:T(8,128)(2,1)S(1)} all-gather(bf16[512,128]{0,1:T(8,128)(2,1)S(1)} %fusion.9), channel_id=1, replica_groups=mesh['ctx'=32,'tp'=4,'dp'=2] {'tp'}, dimensions={0}, use_global_device_ids=true | all-gather | bytes 655360 | tf_op jit(solution)/shard_map/all_gather | solution.py:121
  342.1 82.3 %reduce-scatter.9.cloned.1.call-done = bf16[64,512]{1,0:T(8,128)(2,1)} async-done(((bf16[2048,512]{1,0:T(8,128)(2,1)}), bf16[64,512]{1,0:T(8,128)(2,1)}) %reduce-scatter.9.cloned.1.call-update) | async-done | bytes 65552 | tf_op jit(solution)/shard_map/reduce_scatter | solution.py:125
  425.9 88.1 %reduce-scatter.11.cloned.1.call-done = bf16[48,512]{1,0:T(8,128)(2,1)} async-done(((bf16[1536,512]{1,0:T(8,128)(2,1)}), bf16[48,512]{1,0:T(8,128)(2,1)}) %reduce-scatter.11.cloned.1.call-update) | async-done | bytes 49168 | tf_op jit(solution)/shard_map/reduce_scatter | solution.py:132
  514.0 9.3 %psum.39 = bf16[512,48]{0,1:T(8,128)(2,1)S(1)} all-reduce(bf16[512,48]{0,1:T(8,128)(2,1)} %bitcast.96), channel_id=1, replica_groups=mesh['ctx'=32,'tp'=4,'dp'=2] {'dp'}, use_global_device_ids=true, to_apply=%region_16.17 | all-reduce | flops 24576 | bytes 98304 | tf_op jit(solution)/shard_map/psum | solution.py:142
  523.9 25.9 %all-reduce.3.cloned.1.call-done = bf16[512,64]{0,1:T(8,128)(2,1)} async-done(((bf16[512,64]{0,1:T(8,128)(2,1)}), bf16[512,64]{0,1:T(8,128)(2,1)}) %all-reduce.3.cloned.1.call-update) | async-done | bytes 65552 | tf_op jit(solution)/shard_map/psum | solution.py:141
  (122 shorter events, 70.1 us)
Async XLA Ops:
  7.2 177.4 %copy-start = (bf16[512,2048]{1,0:T(8,128)(2,1)S(1)}, bf16[512,2048]{1,0:T(8,128)(2,1)}, u32[]{:S(2)}) copy-start(bf16[512,2048]{1,0:T(8,128)(2,1)} %param.22) | copy-start | bytes 6291460
  7.2 55.8 %all-gather.9.cloned.1.call-start = ((), (), s32[]{:S(2)}) async-start(), calls=%async_computation.9 | async-start | bytes 4325376 | tf_op jit(solution)/shard_map/all_gather | solution.py:63
  7.9 108.2 %all-gather.11.cloned.1.call-start = ((), (), s32[]{:S(2)}) async-start(), calls=%async_computation.10 | async-start | bytes 4325376 | tf_op jit(solution)/shard_map/all_gather | solution.py:64
  8.7 205.6 %reduce-scatter.7.cloned.1.call-start = ((), (), s32[]{:S(2)}) async-start(), calls=%async_computation.4 | async-start | bytes 655360 | tf_op jit(solution)/shard_map/reduce_scatter | solution.py:80
  183.5 3.1 copy-start.3
  183.5 3.3 copy-start.2
  185.9 76.2 %all-gather.7.cloned.1.call-start = ((), (), s32[]{:S(2)}) async-start(), calls=%async_computation.8 | async-start | bytes 1216512 | tf_op jit(solution)/shard_map/all_gather | solution.py:98
  186.5 105.8 %reduce-scatter.13.cloned.1.call-start = ((), (), s32[]{:S(2)}) async-start(), calls=%async_computation.11 | async-start | bytes 491520
  217.2 207.3 %reduce-scatter.9.cloned.1.call-start = ((), (), s32[]{:S(2)}) async-start(), calls=%async_computation.5 | async-start | bytes 2162688 | tf_op jit(solution)/shard_map/reduce_scatter | solution.py:125
  265.4 54.7 %copy-start.1 = (bf16[512,128]{0,1:T(8,128)(2,1)S(1)}, bf16[512,128]{0,1:T(8,128)(2,1)}, u32[]{:S(2)}) copy-start(bf16[512,128]{0,1:T(8,128)(2,1)} %reduce-scatter.7.cloned.1.call-done) | copy-start | bytes 393220
  340.2 173.8 %reduce-scatter.11.cloned.1.call-start = ((), (), s32[]{:S(2)}) async-start(), calls=%async_computation.7 | async-start | bytes 1622016 | tf_op jit(solution)/shard_map/reduce_scatter | solution.py:132
  342.0 207.7 %all-reduce.3.cloned.1.call-start = ((), (), s32[]{:S(2)}) async-start(), calls=%async_computation.6 | async-start | bytes 131072 | tf_op jit(solution)/shard_map/psum | solution.py:141
Sparse Core Ops, SparseCore 0:
  10.6 52.3 all-gather.8
  65.5 50.5 all-gather.10
  186.0 28.2 reduce-scatter.6
  216.8 45.3 all-gather.6
  264.5 27.6 reduce-scatter.12
  340.3 84.0 reduce-scatter.8
  428.7 85.2 reduce-scatter.10
  516.7 33.0 all-reduce.2
where the time goes:
time: 560 us; the launch traced here: 558 us
  waiting for transfers between devices  398 us (71%)
  blocking collectives  51.7 us (9%)
  local copies, waits for them, and re-layouts  51.4 us (9%)
  matrix products  35.8 us (6%)
  between operations  15 us (3%)
    reduce_scatter x1, waiting for transfers between devices, local(): lax.psum_scatter(lax.dot_general(slab, activation_t, (((1,), (1,)), ((),...  88.1 us
    reduce_scatter x1, waiting for transfers between devices, local(): lax.psum_scatter(jnp.dot(slab, hidden, preferred_element_type=jnp.float32...  82.3 us
    all_gather x1, waiting for transfers between devices, local(): lax.all_gather(attn_values[0], 'ctx', axis=0, tiled=True)  53.1 us
    all_gather x1, waiting for transfers between devices, local(): lax.all_gather(attn_keys[0], 'ctx', axis=0, tiled=True)  48.7 us
    all_gather x1, waiting for transfers between devices, local(): encoder_all = lax.all_gather(enc_feats[0], 'ctx', axis=0, tiled=True)  44.6 us
    dynamic_slice x24, local copies, waits for them, and re-layouts, local(): carry, unused = lax.scan(key_block, carry, (key_blocks, value_blocks))  42.6 us
    unnamed x9, waiting for transfers between devices  28.2 us
    reduce_scatter x1, waiting for transfers between devices, local(): lax.psum_scatter(lax.dot_general(slab, hidden, (((0,), (1,)), ((), ())),...  27.5 us
  transfers between devices with their start and end apart: 8, of which 8 were waited for; matrix products, arithmetic and copies ran while one was open for 3% of the time, Pallas kernels for 0%

commit v1 on v0

v1 whole, which is shorter than its diff:
```python
import functools
import math

import jax
import jax.numpy as jnp
from jax import lax
from jax.experimental import pallas as pl
from jax.experimental.pallas import tpu as pltpu
from jax.sharding import PartitionSpec as P

HD = 128
TOK = 128
eps = 1e-06
loss_scale = 4194304.0
ALL_TOKENS = 8192
BF = jnp.bfloat16
F32 = jnp.float32
MESH = pl.DeviceIdType.MESH
VMEM = pltpu.VMEM


def dot(a, b, ca, cb):
    return lax.dot_general(a, b, (((ca,), (cb,)), ((), ())), preferred_element_type=F32)


def kernel(
    res, q_in, k_in, v_in, gate_in, step, enc, tap_rows, tap_w, win_in, wout_in,
    d_out, gin_out, gout_out,
    qkv, gate, win, wout, encb, osend, ssend, orecv, srecv,
    tgs, tgt, hid, h2, isend, irecv, inner, act, a2, psend, precv, g2, gi2, dacc,
    p1a, p1b, r1a, r1b, s1a, s1b, t1a, t1b, f1, e1,
    p2a, p2b, r2a, r2b, s2a, s2b, t2a, t2b, f2, e2,
    load_sem, qkv_s, qkv_r, enc_s, enc_r, o_s, o_r, st_s, st_r, tg_s, tg_r,
    mate_s, mate_r, i_s, i_r, p_s, p_r, g_s, g_r, gi_s, gi_r, mg_s, mg_r,
    red_s, red_r,
):
    ctx = lax.axis_index("ctx")
    t = lax.axis_index("tp")
    dp = lax.axis_index("dp")
    c = lax.rem(ctx, 2)
    x = lax.rem(lax.div(ctx, 2), 4)
    y = lax.div(ctx, 8)
    me = x * 2 + c
    mine = y * 2 + c

    def at(yy, xx, cc, tt=None, dd=None):
        return {
            "ctx": (yy * 4 + xx) * 2 + cc,
            "tp": t if tt is None else tt,
            "dp": dp if dd is None else dd,
        }

    def up(v, d):
        return lax.rem(v + d, 4)

    mate = at(y, x, 1 - c)
    zpeer = {d: at(y, x, c, tt=up(t, d)) for d in (1, 2, 3)}
    xpeer = {d: at(y, up(x, d), c) for d in (1, 2, 3)}
    ypeer = {d: at(up(y, d), x, c) for d in (1, 2, 3)}

    def send(src, dst, ss, rs, dev):
        cp = pltpu.make_async_remote_copy(
            src_ref=src, dst_ref=dst, send_sem=ss, recv_sem=rs, device_id=dev, device_id_type=MESH
        )
        cp.start()

    def wait(ref, sem):
        pltpu.make_async_copy(ref, ref, sem).wait()

    loads = [
        pltpu.make_async_copy(win_in, win, load_sem.at[0]),
        pltpu.make_async_copy(wout_in, wout, load_sem.at[1]),
        pltpu.make_async_copy(gate_in, gate, load_sem.at[2]),
    ]

    bar = pltpu.get_barrier_semaphore()
    partners = [at(y, up(x, d), cc) for d in (1, 2, 3) for cc in (0, 1)]
    partners += [at(up(y, d), x, cc) for d in (1, 2, 3) for cc in (0, 1)]
    partners += [mate] + [zpeer[d] for d in (1, 2, 3)]
    partners += [at(y, x, cc, dd=1 - dp) for cc in (0, 1)]
    for p in partners:
        pl.semaphore_signal(bar, inc=1, device_id=p, device_id_type=MESH)
    pl.semaphore_wait(bar, len(partners))

    def cols(cc, j):
        return pl.ds(pl.multiple_of(cc * 256 + j * 128, 128), 128)

    for j in (0, 1):
        for n, src, axis in ((1, k_in, 0), (0, q_in, 1), (2, v_in, 0)):
            ss, rs = qkv_s.at[j, n], qkv_r.at[j, n]
            slot = me if axis == 1 else mine
            for d in (2, 1, 3, 0):
                for e in (0, 1):
                    cc = lax.rem(c + e, 2)
                    dst = qkv.at[j, n, slot]
                    if d == 0 and e == 0:
                        pltpu.make_async_copy(src.at[:, cols(cc, j)], dst, rs).start()
                        continue
                    dev = at(y, up(x, d), cc) if axis == 1 else at(up(y, d), x, cc)
                    send(src.at[:, cols(cc, j)], dst, ss, rs, dev)
    pltpu.make_async_copy(enc, encb.at[y, x, c], load_sem.at[3]).start()
    for d in (1, 2, 3):
        send(enc, encb.at[y, x, c], enc_s.at[0], enc_r.at[0], xpeer[d])
    for cp in loads:
        cp.start()

    scale = HD ** (-0.5) * math.log2(math.e)

    def head(j, carry):
        for n in (1, 0, 2):
            wait(qkv.at[j, n], qkv_r.at[j, n])
        keys = qkv[j, 1].reshape(8 * TOK, HD)
        vt = qkv[j, 2].reshape(8 * TOK, HD).T

        def block(it, carry2):
            xq = up(x, 1 + it)
            qb = qkv[j, 0, pl.ds(2 * xq, 2)].reshape(2 * TOK, HD)
            st = dot(keys, qb, 1, 1) * scale
            top = jnp.max(st, axis=0, keepdims=True)
            expo = jnp.exp2(st - top)
            total = jnp.sum(expo, axis=0, keepdims=True)
            ot = dot(vt, expo.astype(BF), 1, 0) / total
            lse = top + jnp.log2(total)
            for cc in (0, 1):
                osend[j, 2 * xq + cc] = ot[:, cc * TOK : (cc + 1) * TOK].astype(BF)
                ssend[2 * xq + cc, j] = jnp.broadcast_to(lse[:, cc * TOK : (cc + 1) * TOK], (8, TOK))
                own = jnp.logical_and(xq == x, cc == c)

                @pl.when(own)
                def _():
                    pltpu.make_async_copy(osend.at[j, 2 * xq + cc], orecv.at[x, c, j], o_r.at[j]).start()

                @pl.when(jnp.logical_not(own))
                def _():
                    send(osend.at[j, 2 * xq + cc], orecv.at[x, c, j], o_s.at[j], o_r.at[j], at(y, xq, cc))
            return carry2

        return lax.fori_loop(0, 4, block, carry)

    lax.fori_loop(0, 2, head, 0)
    for d in (2, 1, 3, 0):
        for cc in (0, 1):
            xq = up(x, d)
            if d == 0:
                @pl.when(cc == c)
                def _():
                    pltpu.make_async_copy(ssend.at[2 * xq + cc], srecv.at[x, c], st_r).start()

                @pl.when(cc != c)
                def _():
                    send(ssend.at[2 * xq + cc], srecv.at[x, c], st_s, st_r, at(y, xq, cc))
            else:
                send(ssend.at[2 * xq + cc], srecv.at[x, c], st_s, st_r, at(y, xq, cc))

    wait(enc, load_sem.at[3])
    wait(encb.at[0, pl.ds(0, 3), 0], enc_r.at[0])
    for d in (2, 1, 3):
        send(encb.at[y, :, c], encb.at[y, :, c], enc_s.at[1], enc_r.at[1], ypeer[d])
    for cp in loads:
        cp.wait()
    pick = (lax.broadcasted_iota(jnp.int32, (16, gate.shape[0]), 1) == step[0]).astype(F32).astype(BF)
    gate_row = dot(pick, gate[...], 1, 0)[0:1]
    base = res[...].astype(F32)

    for j in (0, 1):
        wait(orecv.at[:, :, j], o_r.at[j])
    wait(srecv, st_r)
    for cc in (0, 1):
        for j in (0, 1):
            lses = [srecv[i, cc, j, 0:1, :] for i in range(4)]
            top = jnp.maximum(jnp.maximum(lses[0], lses[1]), jnp.maximum(lses[2], lses[3]))
            ws = [jnp.exp2(v - top) for v in lses]
            inv = 1.0 / (ws[0] + ws[1] + ws[2] + ws[3])
            acc = sum(orecv[i, cc, j].astype(F32) * (ws[i] * inv) for i in range(4))
            lo = (2 * cc + j) * HD
            hid[:, lo : lo + HD] = (
                base[:, lo : lo + HD] + gate_row[:, lo : lo + HD] * acc.T
            ).astype(BF)

    half = pl.ds(pl.multiple_of(c * 256, 256), 256)
    other = pl.ds(pl.multiple_of((1 - c) * 256, 256), 256)

    def slab(tt):
        return pl.ds(pl.multiple_of(tt * 512, 512), 512)

    for d in (2, 1, 3):
        isend[d - 1] = dot(hid[...], win[:, slab(up(t, d))], 1, 0).astype(BF)
        send(isend.at[d - 1], irecv.at[d - 1], i_s, i_r, zpeer[d])
    inner[...] = dot(hid[...], win[:, slab(t)], 1, 0)
    h2[0:TOK] = hid[:, half]
    send(hid.at[:, other], h2.at[pl.ds(TOK, TOK)], mate_s.at[0], mate_r.at[0], mate)

    wait(encb.at[0:3, :, 0], enc_r.at[1])
    send(encb.at[:, :, c], encb.at[:, :, c], enc_s.at[2], enc_r.at[2], mate)
    wait(encb.at[:, :, 0], enc_r.at[2])
    weights = tap_w[...]
    weights = weights / jnp.sum(weights, axis=1, keepdims=True)
    rows = tap_rows[...]
    lane = lax.broadcasted_iota(jnp.int32, (TOK, 1536), 1)
    mix = sum(jnp.where(lane == rows[:, k : k + 1], weights[:, k : k + 1], 0.0) for k in range(4))
    target = dot(mix.astype(BF), encb[...].reshape(1536, 384), 1, 0)
    tgs[...] = target.astype(BF)

    def trows(tt):
        return pl.ds(pl.multiple_of(tt * 32, 32), 32)

    for d in (2, 1, 3):
        send(tgs.at[trows(up(t, d))], tgt.at[t], tg_s, tg_r, zpeer[d])
    tgt[t] = tgs[trows(t)]

    wait(irecv, i_r)
    total = inner[...] + irecv[0].astype(F32) + irecv[1].astype(F32) + irecv[2].astype(F32)
    inner[...] = total
    act[...] = (total / (1.0 + jnp.exp(-total))).astype(BF)
    a2[0:TOK] = act[:, half]
    send(act.at[:, other], a2.at[pl.ds(TOK, TOK)], mate_s.at[1], mate_r.at[1], mate)

    psend[...] = dot(act[...], wout[...], 1, 0).astype(BF)
    for d in (2, 1, 3):
        send(psend.at[trows(up(t, d))], precv.at[d - 1], p_s, p_r, zpeer[d])
    wait(tgt.at[0:3], tg_r)
    wait(precv, p_r)
    proj = psend[trows(t)].astype(F32)
    proj = proj + precv[0].astype(F32) + precv[1].astype(F32) + precv[2].astype(F32)
    tg = jnp.concatenate([tgt[s].astype(F32) for s in range(4)], axis=1)
    norm_p = jnp.sqrt(jnp.sum(proj * proj, axis=1, keepdims=True) + eps)
    norm_t = jnp.sqrt(jnp.sum(tg * tg, axis=1, keepdims=True) + eps)
    cosine = jnp.sum(proj * tg, axis=1, keepdims=True) / (norm_p * norm_t)
    factor = loss_scale / ALL_TOKENS
    g2[trows(t)] = (
        -factor * (tg / (norm_p * norm_t) - cosine * proj / (norm_p * norm_p))
    ).astype(BF)
    for d in (2, 1, 3):
        send(g2.at[trows(t)], g2.at[trows(t)], g_s, g_r, zpeer[d])
    wait(g2.at[0:96], g_r)
    send(g2.at[0:TOK], g2.at[pl.ds(TOK, TOK)], mate_s.at[2], mate_r.at[2], mate)

    grad_act = dot(g2[0:TOK], wout[...], 1, 1)
    v = inner[...]
    sig = 1.0 / (1.0 + jnp.exp(-v))
    gi2[t, 0:TOK] = (grad_act * (sig * (1.0 + v * (1.0 - sig)))).astype(BF)
    for d in (2, 1, 3):
        send(gi2.at[t, pl.ds(0, TOK)], gi2.at[t, pl.ds(0, TOK)], gi_s, gi_r.at[d - 1], zpeer[d])
    send(gi2.at[t, pl.ds(0, TOK)], gi2.at[t, pl.ds(TOK, TOK)], mg_s, mg_r.at[0], mate)

    def stage1_a(pa, ra, k):
        for d in (2, 1, 3):
            send(pa.at[up(y, d)], ra.at[d - 1], red_s.at[k], red_r.at[k], ypeer[d])

    def stage1_b(pb, rb, k):
        for d in (2, 1, 3):
            send(pb.at[:, up(x, d)], rb.at[d - 1], red_s.at[k + 1], red_r.at[k + 1], xpeer[d])

    def stage2(pa, pb, ra, rb, sa, sb, ta, tb, k):
        wait(ra, red_r.at[k])
        sa[...] = (pa[y].astype(F32) + sum(ra[i].astype(F32) for i in range(3))).astype(BF)
        for d in (2, 1, 3):
            send(sa.at[up(x, d)], ta.at[d - 1], red_s.at[k + 2], red_r.at[k + 2], xpeer[d])
        wait(rb, red_r.at[k + 1])
        sb[...] = (pb[:, x].astype(F32) + sum(rb[i].astype(F32) for i in range(3))).astype(BF)
        for d in (2, 1, 3):
            send(sb.at[up(y, d)], tb.at[d - 1], red_s.at[k + 3], red_r.at[k + 3], ypeer[d])

    def stage3(sa, sb, ta, tb, f, ex, k, own):
        wait(ta, red_r.at[k + 2])
        wait(tb, red_r.at[k + 3])
        f[:, 0:128] = (sa[x].astype(F32) + sum(ta[i].astype(F32) for i in range(3))).astype(BF)
        f[:, 128:256] = (sb[y].astype(F32) + sum(tb[i].astype(F32) for i in range(3))).astype(BF)
        mates = pl.ds(pl.multiple_of((1 - c) * own, 16), own)
        ours = pl.ds(pl.multiple_of(c * own, 16), own)
        send(f.at[mates], ex.at[2], red_s.at[k + 4], red_r.at[k + 4], at(y, x, 1 - c, dd=1 - dp))
        send(f.at[ours], ex.at[1], red_s.at[k + 4], red_r.at[k + 4], at(y, x, c, dd=1 - dp))
        send(f.at[mates], ex.at[0], red_s.at[k + 4], red_r.at[k + 4], mate)

    def finish(f, ex, k, own, out):
        wait(ex, red_r.at[k + 4])
        ours = pl.ds(pl.multiple_of(c * own, 16), own)
        here = f[ours].astype(F32) + ex[1].astype(F32)
        there = ex[0].astype(F32) + ex[2].astype(F32)
        out[0:256, :] = jnp.where(c == 0, here, there).T
        out[256:512, :] = jnp.where(c == 0, there, here).T

    for k in (0, 1, 2):
        wait(a2.at[0:TOK] if k < 2 else g2.at[0:TOK], mate_r.at[k])
    for yy in range(4):
        block = dot(g2[:, yy * 384 : (yy + 1) * 384], a2[...], 0, 0).astype(BF)
        p2a[yy] = block[:, 0:128].reshape(4, 96, 128)
        p2b[yy] = block[:, 128:256].reshape(4, 96, 128)
    stage1_a(p2a, r2a, 0)
    stage1_b(p2b, r2b, 0)

    def first(s, start):
        part = dot(gi2[s, 0:TOK], win[:, slab(s)], 1, 1)
        dacc[...] = part if start else dacc[...] + part

    def outer(s, d):
        wait(gi2.at[0, pl.ds(0, TOK)], mg_r.at[d])
        block = dot(gi2[s], h2[...], 0, 0).astype(BF)
        p1a[s] = block[:, 0:128].reshape(4, 128, 128)
        p1b[s] = block[:, 128:256].reshape(4, 128, 128)

    first(t, True)
    outer(t, 0)
    stage2(p2a, p2b, r2a, r2b, s2a, s2b, t2a, t2b, 0)
    for d in (1, 3, 2):
        s = up(t, 4 - d)
        wait(gi2.at[0, pl.ds(0, TOK)], gi_r.at[d - 1])
        send(gi2.at[s, pl.ds(0, TOK)], gi2.at[s, pl.ds(TOK, TOK)], mg_s, mg_r.at[d], mate)
        first(s, False)
        outer(s, d)
        if d == 1:
            stage3(s2a, s2b, t2a, t2b, f2, e2, 0, 48)
    stage1_a(p1a, r1a, 5)
    stage1_b(p1b, r1b, 5)
    d_out[...] = dacc[...].astype(BF)
    finish(f2, e2, 0, 48, gout_out)
    stage2(p1a, p1b, r1a, r1b, s1a, s1b, t1a, t1b, 5)
    stage3(s1a, s1b, t1a, t1b, f1, e1, 5, 64)

    for j in (0, 1):
        for n in (0, 1, 2):
            wait(qkv.at[j, n, pl.ds(0, 7)], qkv_s.at[j, n])
        wait(osend.at[j, pl.ds(0, 7)], o_s.at[j])
    wait(ssend.at[pl.ds(0, 7)], st_s)
    wait(encb.at[0, pl.ds(0, 3), 0], enc_s.at[0])
    wait(encb.at[0:3, :, 0], enc_s.at[1])
    wait(encb.at[:, :, 0], enc_s.at[2])
    wait(tgt.at[0:3], tg_s)
    wait(isend, i_s)
    wait(precv, p_s)
    wait(g2.at[0:96], g_s)
    wait(gi2.at[pl.ds(0, 3), pl.ds(0, TOK)], gi_s)
    wait(gi2.at[:, pl.ds(0, TOK)], mg_s)
    wait(a2.at[0:TOK], mate_s.at[0])
    wait(a2.at[0:TOK], mate_s.at[1])
    wait(g2.at[0:TOK], mate_s.at[2])
    for k, ra, rb, ta, tb, ex in ((0, r2a, r2b, t2a, t2b, e2), (5, r1a, r1b, t1a, t1b, e1)):
        wait(ra, red_s.at[k])
        wait(rb, red_s.at[k + 1])
        wait(ta, red_s.at[k + 2])
        wait(tb, red_s.at[k + 3])
        wait(ex, red_s.at[k + 4])
    finish(f1, e1, 5, 64, gin_out)


def grad_scratch(rows):
    return [
        VMEM((4, 4, rows, 128), BF),
        VMEM((4, 4, rows, 128), BF),
        VMEM((3, 4, rows, 128), BF),
        VMEM((3, 4, rows, 128), BF),
        VMEM((4, rows, 128), BF),
        VMEM((4, rows, 128), BF),
        VMEM((3, rows, 128), BF),
        VMEM((3, rows, 128), BF),
        VMEM((rows, 256), BF),
        VMEM((3, rows // 2, 256), BF),
    ]


def local(
    residual, queries, attn_keys, attn_values, gate_table, timesteps, enc_feats,
    tap_rows, tap_weights, proj_in, proj_out,
):
    dma = pltpu.SemaphoreType.DMA
    vm = pl.BlockSpec(memory_space=VMEM)
    hb = pl.BlockSpec(memory_space=pl.ANY)
    sm = pl.BlockSpec(memory_space=pltpu.SMEM)
    d_hidden, gin, gout = pl.pallas_call(
        kernel,
        name="alignment",
        out_shape=(
            jax.ShapeDtypeStruct((TOK, 512), BF),
            jax.ShapeDtypeStruct((512, 64), F32),
            jax.ShapeDtypeStruct((512, 48), F32),
        ),
        in_specs=[vm, hb, hb, hb, hb, sm, hb, vm, vm, hb, hb],
        out_specs=(vm, vm, vm),
        scratch_shapes=[
            VMEM((2, 3, 8, TOK, HD), BF),
            VMEM((1000, 512), BF),
            VMEM((512, 2048), BF),
            VMEM((512, 1536), BF),
            VMEM((4, 4, 2, 48, 384), BF),
            VMEM((2, 8, HD, TOK), BF),
            VMEM((8, 2, 8, TOK), F32),
            VMEM((4, 2, 2, HD, TOK), BF),
            VMEM((4, 2, 2, 8, TOK), F32),
            VMEM((TOK, 384), BF),
            VMEM((4, 32, 384), BF),
            VMEM((TOK, 512), BF),
            VMEM((2 * TOK, 256), BF),
            VMEM((3, TOK, 512), BF),
            VMEM((3, TOK, 512), BF),
            VMEM((TOK, 512), F32),
            VMEM((TOK, 512), BF),
            VMEM((2 * TOK, 256), BF),
            VMEM((TOK, 1536), BF),
            VMEM((3, 32, 1536), BF),
            VMEM((2 * TOK, 1536), BF),
            VMEM((4, 2 * TOK, 512), BF),
            VMEM((TOK, 512), F32),
            *grad_scratch(128),
            *grad_scratch(96),
            dma((4,)),
            dma((2, 3)),
            dma((2, 3)),
            dma((3,)),
            dma((3,)),
            dma((2,)),
            dma((2,)),
            dma,
            dma,
            dma,
            dma,
            dma((3,)),
            dma((3,)),
            dma,
            dma,
            dma,
            dma,
            dma,
            dma,
            dma,
            dma((3,)),
            dma,
            dma((4,)),
            dma((10,)),
            dma((10,)),
        ],
        compiler_params=pltpu.CompilerParams(
            collective_id=0, has_side_effects=True, vmem_limit_bytes=56 << 20
        ),
        cost_estimate=pl.CostEstimate(
            flops=2_500_000_000, bytes_accessed=16_000_000, transcendentals=2_200_000
        ),
    )(
        residual[0], queries[0], attn_keys[0], attn_values[0], gate_table, timesteps,
        enc_feats[0], tap_rows[0], tap_weights[0], proj_in, proj_out,
    )
    return d_hidden[None], gin, gout


def solution(mesh):
    in_specs = (
        P("dp", "ctx", "tp"),
        P("dp", "ctx", "tp"),
        P("dp", "ctx", "tp"),
        P("dp", "ctx", "tp"),
        P(None, "tp"),
        P("dp"),
        P("dp", "ctx", "tp"),
        P("dp", "ctx", None),
        P("dp", "ctx", None),
        P("tp", None),
        P("tp", None),
    )
    out_specs = (P("dp", "ctx", "tp"), P("tp", "ctx"), P("tp", "ctx"))
    return jax.shard_map(local, mesh=mesh, in_specs=in_specs, out_specs=out_specs, check_vma=False)
```

time: 560 us -> 113 us (0.20)
  waiting for transfers between devices: 398 us -> 0 us
  Pallas kernels: 0 us -> 102 us
  blocking collectives: 51.7 us -> 0 us
  local copies, waits for them, and re-layouts: 51.4 us -> 7.82 us
  matrix products: 35.8 us -> 0 us
  between operations: 15 us -> 1.29 us
    reduce_scatter x3 -> x0, waiting for transfers between devices: 198 us -> none  [the longest x1 88.1 us: local(): lax.psum_scatter(lax.dot_general(slab, activation_t, (((1,), (1,)), ((),...]
    all_gather x3 -> x0, waiting for transfers between devices: 146 us -> none  [the longest x1 53.1 us: local(): lax.all_gather(attn_values[0], 'ctx', axis=0, tiled=True)]
    pallas_call x0 -> x1, Pallas kernels: none -> 102 us  [local(): pl.pallas_call(kernel, name='alignment', out_shape=(jax.ShapeDtypeStruct(...]
    dynamic_slice x24 -> x0, local copies, waits for them, and re-layouts: 42.6 us -> none  [local(): carry, unused = lax.scan(key_block, carry, (key_blocks, value_blocks))]
    dot_general x24 -> x0, matrix products: 35.8 us -> none  [the longest x8 11.5 us: key_block(): jnp.einsum('hqk,khd->hqd', expo.astype(jnp.bfloat16), value_piece, prefer...]
    all_gather x2 -> x0, blocking collectives: 31.5 us -> none  [the longest x1 16 us: local(): inner_full = lax.all_gather(grad_inner_t, 'tp', axis=0, tiled=True)]
    unnamed x9 -> x0, waiting for transfers between devices: 28.2 us -> none
    psum x1 -> x0, waiting for transfers between devices: 25.9 us -> none  [local(): lax.psum(inner_piece, 'dp').astype(jnp.float32)]
  transfers between devices with their start and end apart: 8 -> 0, of which waited for: 8 -> 0; matrix products, arithmetic and copies ran while one was open for 3% -> 0% of each run, Pallas kernels for 0% -> 0%
where the time goes in v1:
time: 113 us; the launch traced here: 111 us
  Pallas kernels  102 us (90%)
  local copies, waits for them, and re-layouts  7.82 us (7%)
  between operations  1.29 us (1%)
    pallas_call x1, Pallas kernels, local(): pl.pallas_call(kernel, name='alignment', out_shape=(jax.ShapeDtypeStruct(...  102 us
    unnamed x5, local copies, waits for them, and re-layouts  7.82 us

profile of v1, /device:TPU:10, one launch (start us, length us, event | category | flops | bytes accessed | tf_op | source)
XLA Modules:
  0.0 111.4 jit_solution(14207721997954926606)
XLA Ops:
  1.3 1.4 %copy.14 = s32[1,128,4]{2,1,0:T(8,128)} copy(s32[1,128,4]{1,2,0:T(4,128)} %param.18) | data formatting | bytes 4096 | tf_op args[7]
  2.7 1.4 %copy.15 = f32[1,128,4]{2,1,0:T(8,128)} copy(f32[1,128,4]{1,2,0:T(4,128)} %param.19) | data formatting | bytes 4096 | tf_op args[8]
  4.1 102.3 %alignment.1 = (bf16[128,512]{1,0:T(8,128)(2,1)}, f32[512,64]{1,0:T(8,128)}, f32[512,48]{1,0:T(8,128)}) custom-call(bf16[128,512]{1,0:T(8,128)(2,1)} %bitcast.11, bf16[128,512]{1,0:T(8,128)(2,1)} %bitcast.12, bf16[128,512]{1,0:T(8,128)(2,1)} %bitcast.13, bf16[128,512]{1,0:T(8,128)(2,1)} %bitcast.14, bf16[1000,512]{1,0:T(8,128)(2,1)} %gate_in.1, ...), custom_call_target="tpu_custom_call" | custom-call | flops 2500000000 | bytes 16000000 | tf_op jit(solution)/shard_map/alignment/pallas_call | solution.py:369
  106.4 1.7 %copy.17 = f32[512,48]{0,1:T(8,128)} copy(f32[512,48]{1,0:T(8,128)} %get-tuple-element.11) | data formatting | bytes 196608
  108.1 1.7 %copy.16 = f32[512,64]{0,1:T(8,128)} copy(f32[512,64]{1,0:T(8,128)} %get-tuple-element.10) | data formatting | bytes 262144
  109.8 1.6 %copy.20 = bf16[1,128,512]{2,1,0:T(8,128)(2,1)} copy(bf16[1,128,512]{2,1,0:T(8,128)(2,1)} %bitcast.8) | data formatting | bytes 262144

commit v2 on v1

v2 whole, which is shorter than its diff:
```python
import functools
import math

import jax
import jax.numpy as jnp
from jax import lax
from jax.experimental import pallas as pl
from jax.experimental.pallas import tpu as pltpu
from jax.sharding import PartitionSpec as P

HD = 128
TOK = 128
eps = 1e-06
loss_scale = 4194304.0
ALL_TOKENS = 8192
BF = jnp.bfloat16
F32 = jnp.float32
MESH = pl.DeviceIdType.MESH
VMEM = pltpu.VMEM


def dot(a, b, ca, cb):
    return lax.dot_general(a, b, (((ca,), (cb,)), ((), ())), preferred_element_type=F32)


def kernel(
    res, q_in, k_in, v_in, gate_in, step, enc, tap_rows, tap_w, win_in, wout_in,
    d_out, gin_out, gout_out,
    qkv, gate, win, wcol, wout, encb, osend, orecv,
    tgs, tgt, hidf, inner, act, a2, psend, precv, g2, gi, gia, dacc,
    p1a, p1b, r1a, r1b, s1a, s1b, t1a, t1b, f1, e1,
    p2a, p2b, r2a, r2b, s2a, s2b, t2a, t2b, f2, e2,
    load_sem, qkv_s, qkv_r, w_s, w_r, enc_s, enc_r, o_s, o_r, tg_s, tg_r,
    mate_s, mate_r, hid_s, hid_r, p_s, p_r, g_s, g_r, gi_s, gi_r, red_s, red_r,
):
    ctx = lax.axis_index("ctx")
    t = lax.axis_index("tp")
    dp = lax.axis_index("dp")
    c = lax.rem(ctx, 2)
    x = lax.rem(lax.div(ctx, 2), 4)
    y = lax.div(ctx, 8)
    me = x * 2 + c
    mine = y * 2 + c

    def at(yy, xx, cc, tt=None, dd=None):
        return {
            "ctx": (yy * 4 + xx) * 2 + cc,
            "tp": t if tt is None else tt,
            "dp": dp if dd is None else dd,
        }

    def up(v, d):
        return lax.rem(v + d, 4)

    mate = at(y, x, 1 - c)
    zpeer = {d: at(y, x, c, tt=up(t, d)) for d in (1, 2, 3)}
    xpeer = {d: at(y, up(x, d), c) for d in (1, 2, 3)}
    ypeer = {d: at(up(y, d), x, c) for d in (1, 2, 3)}

    def send(src, dst, ss, rs, dev):
        cp = pltpu.make_async_remote_copy(
            src_ref=src, dst_ref=dst, send_sem=ss, recv_sem=rs, device_id=dev, device_id_type=MESH
        )
        cp.start()

    def wait(ref, sem):
        pltpu.make_async_copy(ref, ref, sem).wait()

    def cols(cc, j):
        return pl.ds(pl.multiple_of(cc * 256 + j * 128, 128), 128)

    half = pl.ds(pl.multiple_of(c * 256, 256), 256)
    other = pl.ds(pl.multiple_of((1 - c) * 256, 256), 256)

    def slab(tt):
        return pl.ds(pl.multiple_of(tt * 512, 512), 512)

    def trows(h, tt):
        return pl.ds(pl.multiple_of(h * 64 + tt * 16, 16), 16)

    for j in (0, 1):
        for n, src, slot in ((1, k_in, mine), (0, q_in, me), (2, v_in, mine)):
            pltpu.make_async_copy(src.at[:, cols(c, j)], qkv.at[j, n, slot], qkv_r.at[j, n]).start()
    pltpu.make_async_copy(enc, encb.at[y, x, c], load_sem.at[3]).start()
    for cc in (0, 1):
        pltpu.make_async_copy(
            win_in.at[pl.ds(2 * cc, 2), :, slab(t)], wcol.at[t, :, cc], load_sem.at[4]
        ).start()
    loads = [
        pltpu.make_async_copy(gate_in, gate, load_sem.at[2]),
        pltpu.make_async_copy(win_in, win, load_sem.at[0]),
        pltpu.make_async_copy(wout_in, wout, load_sem.at[1]),
    ]
    for cp in loads:
        cp.start()

    bar = pltpu.get_barrier_semaphore()
    partners = [at(y, up(x, d), cc) for d in (1, 2, 3) for cc in (0, 1)]
    partners += [at(up(y, d), x, cc) for d in (1, 2, 3) for cc in (0, 1)]
    partners += [mate, at(y, x, c, dd=1 - dp)]
    near = up(t, 3 - 2 * dp)
    far = up(t, 2)
    partners += [at(y, x, c, tt=near, dd=1 - dp), at(y, x, c, tt=far, dd=1 - dp)]
    partners += [zpeer[d] for d in (2, 1, 3)]
    owner = (t, 2 * c + lax.div(x, 2), lax.rem(x, 2), up(y, t))
    giver = (up(t, 4 - y), 2 * lax.rem(x, 2) + c, lax.div(x, 2), y)
    keeps = jnp.logical_and(
        jnp.logical_and(owner[0] == y, owner[1] == x), jnp.logical_and(owner[2] == c, owner[3] == t)
    )
    for p in reversed(partners):
        pl.semaphore_signal(bar, inc=1, device_id=p, device_id_type=MESH)
    pl.semaphore_signal(
        bar, inc=1, device_id=at(*giver, dd=1 - dp), device_id_type=MESH
    )

    @pl.when(jnp.logical_not(keeps))
    def _():
        pl.semaphore_signal(bar, inc=1, device_id=at(*giver), device_id_type=MESH)

    pl.semaphore_wait(bar, len(partners) + 2 - keeps.astype(jnp.int32))

    for j in (0, 1):
        for n, src, axis in ((1, k_in, 0), (0, q_in, 1), (2, v_in, 0)):
            ss, rs = qkv_s.at[j, n], qkv_r.at[j, n]
            slot = me if axis == 1 else mine
            for d in (2, 1, 3, 0):
                for e in (0, 1):
                    if d == 0 and e == 0:
                        continue
                    cc = lax.rem(c + e, 2)
                    dev = at(y, up(x, d), cc) if axis == 1 else at(up(y, d), x, cc)
                    send(src.at[:, cols(cc, j)], qkv.at[j, n, slot], ss, rs, dev)
        if j == 0:
            for d in (1, 2, 3):
                send(enc, encb.at[y, x, c], enc_s.at[0], enc_r.at[0], xpeer[d])

    send(win_in.at[pl.ds(2 * c, 2), :, slab(near)], wcol.at[t, :, c], w_s.at[0], w_r.at[0],
         at(y, x, c, tt=near, dd=1 - dp))
    send(win_in.at[2 * c + 1 - dp, :, slab(far)], wcol.at[t, 1 - dp, c], w_s.at[1], w_r.at[1],
         at(y, x, c, tt=far, dd=1 - dp))

    for cp in loads:
        cp.wait()
    pick = (lax.broadcasted_iota(jnp.int32, (16, gate.shape[0]), 1) == step[0]).astype(F32).astype(BF)
    gate_row = dot(pick, gate[...], 1, 0)[0:1]
    base = res[...].astype(F32)

    scale = HD ** (-0.5) * math.log2(math.e)

    def keys_of(j):
        for n in (1, 0, 2):
            wait(qkv.at[j, n], qkv_r.at[j, n])
        return qkv[j, 1].reshape(8 * TOK, HD), qkv[j, 2].reshape(8 * TOK, HD).T

    def block(j, h, it, keys, vt):
        xs = (up(x, 1 + 2 * it), up(x, 2 + 2 * it))
        slots = [2 * xq + cc for xq in xs for cc in (0, 1)]
        rows = pl.ds(pl.multiple_of(h * 64, 64), 64)
        qb = jnp.concatenate([qkv[j, 0, s, rows] for s in slots], axis=0)
        st = dot(keys, qb, 1, 1) * scale
        top = jnp.max(st, axis=0, keepdims=True)
        expo = jnp.exp2(st - top)
        total = jnp.sum(expo, axis=0, keepdims=True)
        out = (dot(vt, expo.astype(BF), 1, 0) / total).T.astype(BF)
        lse = top + jnp.log2(total)
        high = lse.astype(BF).astype(F32)
        mid = (lse - high).astype(BF).astype(F32)
        line = lax.broadcasted_iota(jnp.int32, (16, 256), 0)
        lses = jnp.where(line == 0, high, jnp.where(line == 1, mid, lse - high - mid)).astype(BF)
        for k, slot in enumerate(slots):
            xq, cc = xs[k // 2], k % 2
            osend[j, h, slot, 0:64] = out[64 * k : 64 * k + 64]
            osend[j, h, slot, 64:80] = lses[:, 128 * (k // 2) : 128 * (k // 2) + 128]
            own = jnp.logical_and(xq == x, cc == c)

            @pl.when(own)
            def _():
                pltpu.make_async_copy(osend.at[j, h, slot], orecv.at[h, x, c, j], o_r.at[j, h]).start()

            @pl.when(jnp.logical_not(own))
            def _():
                send(osend.at[j, h, slot], orecv.at[h, x, c, j], o_s.at[j, h], o_r.at[j, h], at(y, xq, cc))

    def combine(j, h):
        wait(orecv.at[h, :, :, j], o_r.at[j, h])
        lses = [
            jnp.concatenate(
                [
                    jnp.sum(orecv[h, i, cc, j, 64:80].astype(F32)[0:3], axis=0, keepdims=True)
                    for cc in (0, 1)
                ],
                axis=0,
            )
            for i in range(4)
        ]
        top = jnp.maximum(jnp.maximum(lses[0], lses[1]), jnp.maximum(lses[2], lses[3]))
        ws = [jnp.exp2(v - top) for v in lses]
        inv = 1.0 / (ws[0] + ws[1] + ws[2] + ws[3])
        wt = jnp.concatenate([w * inv for w in ws], axis=0).T
        wt = jnp.where(c == 0, wt[0:64], wt[64:128])
        r = 64 * h
        for cc in (0, 1):
            acc = sum(
                orecv[h, i, cc, j, 0:64].astype(F32) * wt[:, 2 * i + cc : 2 * i + cc + 1] for i in range(4)
            )
            lo = (2 * cc + j) * HD
            hidf[t, j, r : r + 64, cc * HD : cc * HD + HD] = (
                base[r : r + 64, lo : lo + HD] + gate_row[:, lo : lo + HD] * acc
            ).astype(BF)

    def share(j, rows, k):
        for d in (2, 1, 3):
            send(hidf.at[t, j, rows], hidf.at[t, j, rows], hid_s.at[k], hid_r.at[k], zpeer[d])

    keys, vt = keys_of(0)
    for h in (0, 1):

        def loop0(it, carry):
            block(0, h, it, keys, vt)
            return carry

        lax.fori_loop(0, 2, loop0, 0)
        pair = at(y, x, c, dd=1 - dp)
        if h == 0:
            wait(wcol.at[0, :, 0], w_r.at[0])
            send(wcol.at[near, :, c], wcol.at[near, :, c], w_s.at[2], w_r.at[2], pair)
        else:
            wait(wcol.at[0, 0, 0], w_r.at[1])
            send(wcol.at[far, dp, c], wcol.at[far, dp, c], w_s.at[3], w_r.at[3], pair)

    wait(enc, load_sem.at[3])
    wait(encb.at[0, pl.ds(0, 3), 0], enc_r.at[0])
    for d in (2, 1, 3):
        send(encb.at[y, :, c], encb.at[y, :, c], enc_s.at[1], enc_r.at[1], ypeer[d])

    keys1, vt1 = keys_of(1)
    for h in (0, 1):

        def loop1(it, carry):
            block(1, h, it, keys1, vt1)
            return carry

        lax.fori_loop(0, 2, loop1, 0)
        if h == 0:
            combine(0, 0)
            combine(0, 1)
            share(0, pl.ds(0, TOK), 0)
    combine(1, 0)
    share(1, pl.ds(0, 64), 1)

    wait(wcol.at[0, :, 0], w_r.at[2])
    wait(wcol.at[0, 0, 0], w_r.at[3])
    for d in (1, 2, 3):
        s = up(t, d)
        send(wcol.at[s, :, c], wcol.at[s, :, c], w_s.at[4], w_r.at[4], mate)
    wait(encb.at[0:3, :, 0], enc_r.at[1])
    send(encb.at[:, :, c], encb.at[:, :, c], enc_s.at[2], enc_r.at[2], mate)
    combine(1, 1)
    share(1, pl.ds(64, 64), 2)

    def first_end(h):
        rows = pl.ds(64 * h, 64)
        wait(hidf.at[pl.ds(0, 3), 1, pl.ds(0, 64)], hid_r.at[1 + h])
        total = inner[rows] + sum(
            dot(hidf[s, 1, rows], wcol[s, 1].reshape(256, 512), 1, 0) for s in range(4)
        )
        inner[rows] = total
        act[rows] = (total / (1.0 + jnp.exp(-total))).astype(BF)

    def last_start(h):
        rows = pl.ds(64 * h, 64)
        psend[rows] = dot(act[rows], wout[...], 1, 0).astype(BF)
        for d in (2, 1, 3):
            send(psend.at[trows(h, up(t, d))], precv.at[h, d - 1], p_s.at[h], p_r.at[h], zpeer[d])

    def loss(h):
        wait(tgt.at[h, pl.ds(0, 3)], tg_r.at[h])
        tg = jnp.concatenate([tgt[h, s].astype(F32) for s in range(4)], axis=1)
        norm_t = jnp.sqrt(jnp.sum(tg * tg, axis=1, keepdims=True) + eps)
        wait(precv.at[h], p_r.at[h])
        proj = psend[trows(h, t)].astype(F32) + sum(precv[h, i].astype(F32) for i in range(3))
        norm_p = jnp.sqrt(jnp.sum(proj * proj, axis=1, keepdims=True) + eps)
        cosine = jnp.sum(proj * tg, axis=1, keepdims=True) / (norm_p * norm_t)
        factor = loss_scale / ALL_TOKENS
        own = trows(h, t)
        g2[own] = (-factor * (tg / (norm_p * norm_t) - cosine * proj / (norm_p * norm_p))).astype(BF)
        for d in (2, 1, 3):
            send(g2.at[own], g2.at[own], g_s.at[h], g_r.at[h], zpeer[d])

    def hidden_grad(h):
        rows = pl.ds(64 * h, 64)
        mrows = pl.ds(TOK + 64 * h, 64)
        wait(g2.at[0:48], g_r.at[h])
        send(g2.at[rows], g2.at[mrows], mate_s.at[2 + h], mate_r.at[2 + h], mate)
        v = inner[rows]
        sig = 1.0 / (1.0 + jnp.exp(-v))
        grad_act = dot(g2[rows], wout[...], 1, 1)
        gi[t, rows] = (grad_act * (sig * (1.0 + v * (1.0 - sig)))).astype(BF)
        for d in (2, 1, 3):
            send(gi.at[t, rows], gi.at[t, rows], gi_s, gi_r.at[d - 1], zpeer[d])
        send(gi.at[t, rows, other], gia.at[mrows], mate_s.at[4 + h], mate_r.at[4 + h], mate)

    weights = tap_w[...]
    weights = weights / jnp.sum(weights, axis=0, keepdims=True)
    taps = jnp.concatenate([tap_rows[...].astype(F32), weights], axis=0).T
    rows, weights = taps[:, 0:4], taps[:, 4:8]
    lane = lax.broadcasted_iota(jnp.int32, (TOK, 1536), 1).astype(F32)
    mix = sum(jnp.where(lane == rows[:, k : k + 1], weights[:, k : k + 1], 0.0) for k in range(4))
    wait(encb.at[:, :, 0], enc_r.at[2])
    tgs[...] = dot(mix.astype(BF), encb[...].reshape(1536, 384), 1, 0).astype(BF)
    for h in (0, 1):
        for d in (2, 1, 3):
            send(tgs.at[trows(h, up(t, d))], tgt.at[h, t], tg_s.at[h], tg_r.at[h], zpeer[d])
        tgt[h, t] = tgs[trows(h, t)]

    wait(wcol.at[0], load_sem.at[4])
    wait(wcol.at[pl.ds(0, 3), :, 0], w_r.at[4])
    wait(hidf.at[pl.ds(0, 3), 0, pl.ds(0, TOK)], hid_r.at[0])
    inner[...] = sum(dot(hidf[s, 0, 0:TOK], wcol[s, 0].reshape(256, 512), 1, 0) for s in range(4))
    for h in (0, 1):
        first_end(h)
        last_start(h)
    send(hidf.at[:, :, pl.ds(0, TOK)], hidf.at[:, :, pl.ds(TOK, TOK)], mate_s.at[0], mate_r.at[0], mate)
    a2[0:TOK] = act[:, half]
    send(act.at[:, other], a2.at[pl.ds(TOK, TOK)], mate_s.at[1], mate_r.at[1], mate)
    for h in (0, 1):
        loss(h)
    for h in (0, 1):
        hidden_grad(h)

    wait(a2.at[0:TOK], mate_r.at[1])
    for h in (0, 1):
        wait(g2.at[0:64], mate_r.at[2 + h])
    for yy in range(4):
        part = dot(g2[:, yy * 384 : (yy + 1) * 384], a2[...], 0, 0).astype(BF)
        p2a[yy] = part[:, 0:128].reshape(4, 96, 128)
        p2b[yy] = part[:, 128:256].reshape(4, 96, 128)
    gia[0:TOK] = gi[t, :, half]
    wait(hidf.at[:, :, pl.ds(0, TOK)], mate_r.at[0])
    for h in (0, 1):
        wait(gia.at[0:64], mate_r.at[4 + h])
    for d in (2, 1, 3, 0):
        s = up(up(y, d), t)
        p1a[s] = dot(gia[...], hidf[s, 0], 0, 0).astype(BF)
        p1b[:, s] = dot(gia[...], hidf[s, 1], 0, 0).astype(BF).reshape(4, 64, 256)
        if d:
            send(p1a.at[s], r1a.at[d - 1], red_s.at[0], red_r.at[0], ypeer[d])
    for d in (2, 1, 3):
        send(p1b.at[up(x, d)], r1b.at[d - 1], red_s.at[1], red_r.at[1], xpeer[d])
    for d in (2, 1, 3):
        send(p2a.at[up(y, d)], r2a.at[d - 1], red_s.at[5], red_r.at[5], ypeer[d])
        send(p2b.at[:, up(x, d)], r2b.at[d - 1], red_s.at[6], red_r.at[6], xpeer[d])

    def first(s, start):
        part = dot(gi[s], win[:, :, slab(s)].reshape(512, 512), 1, 1)
        dacc[...] = part if start else dacc[...] + part

    first(t, True)

    block_mine = up(y, t)
    wait(r1a, red_r.at[0])
    total = p1a[block_mine].astype(F32) + sum(r1a[i].astype(F32) for i in range(3))
    s1a[...] = total.astype(BF).reshape(4, 64, 256)
    for d in (2, 1, 3):
        send(s1a.at[up(x, d)], t1a.at[d - 1], red_s.at[2], red_r.at[2], xpeer[d])
    wait(r1b, red_r.at[1])
    s1b[...] = (p1b[x].astype(F32) + sum(r1b[i].astype(F32) for i in range(3))).astype(BF)
    for d in (2, 1, 3):
        send(s1b.at[up(up(y, d), t)], t1b.at[d - 1], red_s.at[3], red_r.at[3], ypeer[d])

    wait(r2a, red_r.at[5])
    s2a[...] = (p2a[y].astype(F32) + sum(r2a[i].astype(F32) for i in range(3))).astype(BF)
    wait(r2b, red_r.at[6])
    s2b[...] = (p2b[:, x].astype(F32) + sum(r2b[i].astype(F32) for i in range(3))).astype(BF)
    for d in (2, 1, 3, 0):
        for e in (0, 1):
            cc = lax.rem(c + e, 2)
            part = pl.ds(pl.multiple_of(cc * 48, 16), 48)
            xq, yq = up(x, d), up(y, d)
            if d == 0 and e == 0:
                pltpu.make_async_copy(s2a.at[x, part], t2a.at[c, x], red_r.at[7]).start()
                pltpu.make_async_copy(s2b.at[y, part], t2b.at[c, y], red_r.at[8]).start()
            else:
                k = 7 if d else 8
                send(s2a.at[xq, part], t2a.at[c, x], red_s.at[k], red_r.at[7], at(y, xq, cc))
                send(s2b.at[yq, part], t2b.at[c, y], red_s.at[k], red_r.at[8], at(yq, x, cc))

    wait(t1a, red_r.at[2])
    f1[0] = (s1a[x].astype(F32) + sum(t1a[i].astype(F32) for i in range(3))).astype(BF)
    wait(t1b, red_r.at[3])
    f1[1] = (s1b[block_mine].astype(F32) + sum(t1b[i].astype(F32) for i in range(3))).astype(BF)
    send(f1, e1.at[dp], red_s.at[4], red_r.at[4], at(*owner, dd=1 - dp))

    @pl.when(keeps)
    def _():
        pltpu.make_async_copy(f1, e1.at[dp], red_r.at[4]).start()

    @pl.when(jnp.logical_not(keeps))
    def _():
        send(f1, e1.at[dp], red_s.at[4], red_r.at[4], at(*owner))

    wait(t2a, red_r.at[7])
    wait(t2b, red_r.at[8])
    for cc in (0, 1):
        for n, f in enumerate((t2a, t2b)):
            total = sum(f[cc, i].astype(F32) for i in range(4))
            f2[:, 256 * cc + 128 * n : 256 * cc + 128 * n + 128] = total.astype(BF)
    send(f2, e2, red_s.at[9], red_r.at[9], pair)

    for d in (1, 3, 2):
        s = up(t, 4 - d)
        wait(gi.at[0], gi_r.at[d - 1])
        first(s, False)
    d_out[...] = dacc[...].astype(BF)

    for j in (0, 1):
        for n in (0, 1, 2):
            wait(qkv.at[j, n, pl.ds(0, 7)], qkv_s.at[j, n])
        for h in (0, 1):
            wait(osend.at[j, h, pl.ds(0, 7)], o_s.at[j, h])
    wait(wcol.at[0, :, 0], w_s.at[0])
    wait(wcol.at[0, 0, 0], w_s.at[1])
    wait(wcol.at[0, :, 0], w_s.at[2])
    wait(wcol.at[0, 0, 0], w_s.at[3])
    wait(wcol.at[pl.ds(0, 3), :, 0], w_s.at[4])
    wait(encb.at[0, pl.ds(0, 3), 0], enc_s.at[0])
    wait(encb.at[0:3, :, 0], enc_s.at[1])
    wait(encb.at[:, :, 0], enc_s.at[2])
    wait(hidf.at[pl.ds(0, 3), 0, pl.ds(0, TOK)], hid_s.at[0])
    wait(hidf.at[:, :, pl.ds(0, TOK)], mate_s.at[0])
    wait(a2.at[0:TOK], mate_s.at[1])
    for h in (0, 1):
        wait(hidf.at[pl.ds(0, 3), 1, pl.ds(0, 64)], hid_s.at[1 + h])
        wait(tgt.at[h, pl.ds(0, 3)], tg_s.at[h])
        wait(precv.at[h], p_s.at[h])
        wait(g2.at[0:48], g_s.at[h])
        wait(g2.at[0:64], mate_s.at[2 + h])
        wait(gia.at[0:64], mate_s.at[4 + h])
    wait(gi.at[pl.ds(0, 3)], gi_s)
    wait(r1a, red_s.at[0])
    wait(r1b, red_s.at[1])
    wait(t1a, red_s.at[2])
    wait(t1b, red_s.at[3])
    wait(r2a, red_s.at[5])
    wait(r2b, red_s.at[6])
    wait(r2a.at[:, pl.ds(0, 2)], red_s.at[7])
    wait(s2a.at[0], red_s.at[8])
    wait(f2, red_s.at[9])

    @pl.when(keeps)
    def _():
        wait(f1, red_s.at[4])

    @pl.when(jnp.logical_not(keeps))
    def _():
        wait(e1, red_s.at[4])

    wait(e2, red_r.at[9])
    gout_out[...] = f2[...].astype(F32) + e2[...].astype(F32)
    wait(e1, red_r.at[4])
    for j in (0, 1):
        total = e1[0, j].astype(F32) + e1[1, j].astype(F32)
        for cc in (0, 1):
            lo = (2 * cc + j) * HD
            gin_out[:, lo : lo + HD] = total[:, cc * HD : cc * HD + HD]


def keep(a, b, c, a_out, b_out, c_out):
    a_out[...] = a[...]
    b_out[...] = b[...]
    c_out[...] = c[...]


def local(
    residual, queries, attn_keys, attn_values, gate_table, timesteps, enc_feats,
    tap_rows, tap_weights, proj_in, proj_out,
):
    dma = pltpu.SemaphoreType.DMA
    vm = pl.BlockSpec(memory_space=VMEM)
    hb = pl.BlockSpec(memory_space=pl.ANY)
    sm = pl.BlockSpec(memory_space=pltpu.SMEM)
    d_hidden, gin, gout = pl.pallas_call(
        kernel,
        name="alignment",
        out_shape=(
            jax.ShapeDtypeStruct((TOK, 512), BF),
            jax.ShapeDtypeStruct((64, 512), F32),
            jax.ShapeDtypeStruct((48, 512), F32),
        ),
        in_specs=[vm, hb, hb, hb, hb, sm, hb, vm, vm, hb, hb],
        out_specs=(vm, vm, vm),
        scratch_shapes=[
            VMEM((2, 3, 8, TOK, HD), BF),
            VMEM((1000, 512), BF),
            VMEM((4, HD, 2048), BF),
            VMEM((4, 2, 2, HD, 512), BF),
            VMEM((512, 1536), BF),
            VMEM((4, 4, 2, 48, 384), BF),
            VMEM((2, 2, 8, 80, HD), BF),
            VMEM((2, 4, 2, 2, 80, HD), BF),
            VMEM((TOK, 384), BF),
            VMEM((2, 4, 16, 384), BF),
            VMEM((4, 2, 2 * TOK, 256), BF),
            VMEM((TOK, 512), F32),
            VMEM((TOK, 512), BF),
            VMEM((2 * TOK, 256), BF),
            VMEM((TOK, 1536), BF),
            VMEM((2, 3, 16, 1536), BF),
            VMEM((2 * TOK, 1536), BF),
            VMEM((4, TOK, 512), BF),
            VMEM((2 * TOK, 256), BF),
            VMEM((TOK, 512), F32),
            VMEM((4, 256, 256), BF),
            VMEM((4, 4, 64, 256), BF),
            VMEM((3, 256, 256), BF),
            VMEM((3, 4, 64, 256), BF),
            VMEM((4, 64, 256), BF),
            VMEM((4, 64, 256), BF),
            VMEM((3, 64, 256), BF),
            VMEM((3, 64, 256), BF),
            VMEM((2, 64, 256), BF),
            VMEM((2, 2, 64, 256), BF),
            VMEM((4, 4, 96, 128), BF),
            VMEM((4, 4, 96, 128), BF),
            VMEM((3, 4, 96, 128), BF),
            VMEM((3, 4, 96, 128), BF),
            VMEM((4, 96, 128), BF),
            VMEM((4, 96, 128), BF),
            VMEM((2, 4, 48, 128), BF),
            VMEM((2, 4, 48, 128), BF),
            VMEM((48, 512), BF),
            VMEM((48, 512), BF),
            dma((5,)),
            dma((2, 3)),
            dma((2, 3)),
            dma((5,)),
            dma((5,)),
            dma((3,)),
            dma((3,)),
            dma((2, 2)),
            dma((2, 2)),
            dma((2,)),
            dma((2,)),
            dma((6,)),
            dma((6,)),
            dma((3,)),
            dma((3,)),
            dma((2,)),
            dma((2,)),
            dma((2,)),
            dma((2,)),
            dma,
            dma((3,)),
            dma((10,)),
            dma((10,)),
        ],
        compiler_params=pltpu.CompilerParams(
            collective_id=0, has_side_effects=True, vmem_limit_bytes=56 << 20
        ),
        cost_estimate=pl.CostEstimate(
            flops=2_500_000_000, bytes_accessed=16_000_000, transcendentals=2_200_000
        ),
    )(
        residual[0], queries[0], attn_keys[0], attn_values[0], gate_table, timesteps,
        enc_feats[0], tap_rows[0].T, tap_weights[0].T, proj_in.reshape(4, HD, 2048), proj_out,
    )
    d_hidden, gin, gout = pl.pallas_call(
        keep,
        name="keep",
        out_shape=(
            jax.ShapeDtypeStruct((TOK, 512), BF),
            jax.ShapeDtypeStruct((64, 512), F32),
            jax.ShapeDtypeStruct((48, 512), F32),
        ),
        in_specs=[vm, vm, vm],
        out_specs=(vm, vm, vm),
    )(d_hidden, gin, gout)
    return d_hidden[None], gin.T, gout.T


def solution(mesh):
    in_specs = (
        P("dp", "ctx", "tp"),
        P("dp", "ctx", "tp"),
        P("dp", "ctx", "tp"),
        P("dp", "ctx", "tp"),
        P(None, "tp"),
        P("dp"),
        P("dp", "ctx", "tp"),
        P("dp", "ctx", None),
        P("dp", "ctx", None),
        P("tp", None),
        P("tp", None),
    )
    out_specs = (P("dp", "ctx", "tp"), P("tp", "ctx"), P("tp", "ctx"))
    return jax.shard_map(local, mesh=mesh, in_specs=in_specs, out_specs=out_specs, check_vma=False)
```

time: 113 us -> 102 us (0.903); the launches traced: 111 us -> 102 us
  local copies, waits for them, and re-layouts: 7.82 us -> 0 us
  Pallas kernels: 102 us -> 100 us
    unnamed x5 -> x0, local copies, waits for them, and re-layouts: 7.82 us -> none
    pallas_call x1, Pallas kernels: 102 us -> 98.6 us  [local(): pl.pallas_call(kernel, name='alignment', out_shape=(jax.ShapeDtypeStruct(...]
    pallas_call x0 -> x1, Pallas kernels: none -> 1.76 us  [local(): pl.pallas_call(keep, name='keep', out_shape=(jax.ShapeDtypeStruct((TOK, 5...]
where the time goes in v2:
time: 102 us
  Pallas kernels  100 us (98%)
  between operations  1.29 us (1%)
    pallas_call x1, Pallas kernels, local(): pl.pallas_call(kernel, name='alignment', out_shape=(jax.ShapeDtypeStruct(...  98.6 us

profile of v2, /device:TPU:10, one launch (start us, length us, event | category | flops | bytes accessed | tf_op | source)
XLA Modules:
  0.0 101.7 jit_solution(3916644620430908166)
XLA Ops:
  1.3 98.6 %alignment.1 = (bf16[128,512]{1,0:T(8,128)(2,1)}, f32[64,512]{1,0:T(8,128)}, f32[48,512]{1,0:T(8,128)}) custom-call(bf16[128,512]{1,0:T(8,128)(2,1)} %bitcast.16, bf16[128,512]{1,0:T(8,128)(2,1)} %bitcast.17, bf16[128,512]{1,0:T(8,128)(2,1)} %bitcast.18, bf16[128,512]{1,0:T(8,128)(2,1)} %bitcast.19, bf16[1000,512]{1,0:T(8,128)(2,1)} %gate_in.1, ...), custom_call_target="tpu_custom_call" | custom-call | flops 2500000000 | bytes 16000000 | tf_op jit(solution)/shard_map/alignment/pallas_call | solution.py:482
  99.9 1.8 %keep.1 = (bf16[128,512]{1,0:T(8,128)(2,1)}, f32[64,512]{1,0:T(8,128)}, f32[48,512]{1,0:T(8,128)}) custom-call(bf16[128,512]{1,0:T(8,128)(2,1)} %get-tuple-element.9.a, f32[64,512]{1,0:T(8,128)} %get-tuple-element.10.b, f32[48,512]{1,0:T(8,128)} %get-tuple-element.11.c), custom_call_target="tpu_custom_call" | custom-call | tf_op jit(solution)/shard_map/keep/pallas_call | solution.py:567

commit v3 on v2

--- a/solution.py
+++ b/solution.py
@@ -27,10 +27,10 @@
     res, q_in, k_in, v_in, gate_in, step, enc, tap_rows, tap_w, win_in, wout_in,
     d_out, gin_out, gout_out,
     qkv, gate, win, wcol, wout, encb, osend, orecv,
-    tgs, tgt, hidf, inner, act, a2, psend, precv, g2, gi, gia, dacc,
+    scores, tops, tgs, tgt, hidf, inner, act, a2, psend, precv, g2, gi, gia, dacc,
     p1a, p1b, r1a, r1b, s1a, s1b, t1a, t1b, f1, e1,
     p2a, p2b, r2a, r2b, s2a, s2b, t2a, t2b, f2, e2,
-    load_sem, qkv_s, qkv_r, w_s, w_r, enc_s, enc_r, o_s, o_r, tg_s, tg_r,
+    load_sem, qkv_s, qkv_r, kv_s, kv_r, w_s, w_r, enc_s, enc_r, o_s, o_r, tg_s, tg_r,
     mate_s, mate_r, hid_s, hid_r, p_s, p_r, g_s, g_r, gi_s, gi_r, red_s, red_r,
 ):
     ctx = lax.axis_index("ctx")
@@ -119,25 +119,30 @@
 
     pl.semaphore_wait(bar, len(partners) + 2 - keeps.astype(jnp.int32))
 
-    for j in (0, 1):
-        for n, src, axis in ((1, k_in, 0), (0, q_in, 1), (2, v_in, 0)):
-            ss, rs = qkv_s.at[j, n], qkv_r.at[j, n]
-            slot = me if axis == 1 else mine
-            for d in (2, 1, 3, 0):
-                for e in (0, 1):
-                    if d == 0 and e == 0:
-                        continue
-                    cc = lax.rem(c + e, 2)
-                    dev = at(y, up(x, d), cc) if axis == 1 else at(up(y, d), x, cc)
-                    send(src.at[:, cols(cc, j)], qkv.at[j, n, slot], ss, rs, dev)
-        if j == 0:
-            for d in (1, 2, 3):
-                send(enc, encb.at[y, x, c], enc_s.at[0], enc_r.at[0], xpeer[d])
-
     send(win_in.at[pl.ds(2 * c, 2), :, slab(near)], wcol.at[t, :, c], w_s.at[0], w_r.at[0],
          at(y, x, c, tt=near, dd=1 - dp))
     send(win_in.at[2 * c + 1 - dp, :, slab(far)], wcol.at[t, 1 - dp, c], w_s.at[1], w_r.at[1],
          at(y, x, c, tt=far, dd=1 - dp))
+
+    above, below = up(y, 1), up(y, 3)
+    for j in (0, 1):
+        for n, src, step_y, rs in (
+            (1, k_in, 1, kv_r.at[j, 0]),
+            (2, v_in, 3, kv_r.at[j, 1]),
+            (1, k_in, 3, qkv_r.at[j, 1]),
+            (2, v_in, 1, qkv_r.at[j, 2]),
+        ):
+            for cc in (0, 1):
+                send(src.at[:, cols(cc, j)], qkv.at[j, n, mine], qkv_s.at[j, n], rs, at(up(y, step_y), x, cc))
+        for n, src in ((1, k_in), (2, v_in)):
+            send(src.at[:, cols(1 - c, j)], qkv.at[j, n, mine], qkv_s.at[j, n], qkv_r.at[j, n], mate)
+        for d in (2, 1, 3):
+            for cc in (0, 1):
+                send(q_in.at[:, cols(cc, j)], qkv.at[j, 0, me], qkv_s.at[j, 0], qkv_r.at[j, 0], at(y, up(x, d), cc))
+        send(q_in.at[:, cols(1 - c, j)], qkv.at[j, 0, me], qkv_s.at[j, 0], qkv_r.at[j, 0], mate)
+        if j == 0:
+            for d in (1, 2, 3):
+                send(enc, encb.at[y, x, c], enc_s.at[0], enc_r.at[0], xpeer[d])
 
     for cp in loads:
         cp.wait()
@@ -147,19 +152,37 @@
 
     scale = HD ** (-0.5) * math.log2(math.e)
 
+    def relay(j):
+        wait(qkv.at[j, 1, pl.ds(0, 2)], kv_r.at[j, 0])
+        low = pl.ds(2 * below, 2)
+        send(qkv.at[j, 1, low], qkv.at[j, 1, low], kv_s.at[j, 0], qkv_r.at[j, 1], at(above, x, c))
+        wait(qkv.at[j, 2, pl.ds(0, 2)], kv_r.at[j, 1])
+        high = pl.ds(2 * above, 2)
+        send(qkv.at[j, 2, high], qkv.at[j, 2, high], kv_s.at[j, 1], qkv_r.at[j, 2], at(below, x, c))
+
     def keys_of(j):
-        for n in (1, 0, 2):
-            wait(qkv.at[j, n], qkv_r.at[j, n])
+        wait(qkv.at[j, 0], qkv_r.at[j, 0])
+        wait(qkv.at[j, 1, pl.ds(0, 6)], qkv_r.at[j, 1])
+        wait(qkv.at[j, 2, pl.ds(0, 6)], qkv_r.at[j, 2])
         return qkv[j, 1].reshape(8 * TOK, HD), qkv[j, 2].reshape(8 * TOK, HD).T
 
-    def block(j, h, it, keys, vt):
+    def produce(j, n, keys):
+        h, it = lax.div(n, 2), lax.rem(n, 2)
         xs = (up(x, 1 + 2 * it), up(x, 2 + 2 * it))
         slots = [2 * xq + cc for xq in xs for cc in (0, 1)]
         rows = pl.ds(pl.multiple_of(h * 64, 64), 64)
         qb = jnp.concatenate([qkv[j, 0, s, rows] for s in slots], axis=0)
-        st = dot(keys, qb, 1, 1) * scale
-        top = jnp.max(st, axis=0, keepdims=True)
-        expo = jnp.exp2(st - top)
+        st = dot(keys, qb, 1, 1)
+        scores[lax.rem(n, 2)] = st
+        tops[lax.rem(n, 2)] = jnp.broadcast_to(jnp.max(st, axis=0, keepdims=True), (8, 256))
+
+    def consume(j, n, vt):
+        h, it = lax.div(n, 2), lax.rem(n, 2)
+        top = tops[lax.rem(n, 2), 0:1]
+        expo = jnp.exp2((scores[lax.rem(n, 2)] - top) * scale)
+        top = top * scale
+        xs = (up(x, 1 + 2 * it), up(x, 2 + 2 * it))
+        slots = [2 * xq + cc for xq in xs for cc in (0, 1)]
         total = jnp.sum(expo, axis=0, keepdims=True)
         out = (dot(vt, expo.astype(BF), 1, 0) / total).T.astype(BF)
         lse = top + jnp.log2(total)
@@ -168,9 +191,15 @@
         line = lax.broadcasted_iota(jnp.int32, (16, 256), 0)
         lses = jnp.where(line == 0, high, jnp.where(line == 1, mid, lse - high - mid)).astype(BF)
         for k, slot in enumerate(slots):
-            xq, cc = xs[k // 2], k % 2
             osend[j, h, slot, 0:64] = out[64 * k : 64 * k + 64]
             osend[j, h, slot, 64:80] = lses[:, 128 * (k // 2) : 128 * (k // 2) + 128]
+
+    def give(j, n):
+        h, it = lax.div(n, 2), lax.rem(n, 2)
+        xs = (up(x, 1 + 2 * it), up(x, 2 + 2 * it))
+        for k in range(4):
+            xq, cc = xs[k // 2], k % 2
+            slot = 2 * xq + cc
             own = jnp.logical_and(xq == x, cc == c)
 
             @pl.when(own)
@@ -212,41 +241,49 @@
         for d in (2, 1, 3):
             send(hidf.at[t, j, rows], hidf.at[t, j, rows], hid_s.at[k], hid_r.at[k], zpeer[d])
 
+    pair = at(y, x, c, dd=1 - dp)
+    relay(0)
+    relay(1)
     keys, vt = keys_of(0)
-    for h in (0, 1):
-
-        def loop0(it, carry):
-            block(0, h, it, keys, vt)
-            return carry
-
-        lax.fori_loop(0, 2, loop0, 0)
-        pair = at(y, x, c, dd=1 - dp)
-        if h == 0:
-            wait(wcol.at[0, :, 0], w_r.at[0])
-            send(wcol.at[near, :, c], wcol.at[near, :, c], w_s.at[2], w_r.at[2], pair)
-        else:
-            wait(wcol.at[0, 0, 0], w_r.at[1])
-            send(wcol.at[far, dp, c], wcol.at[far, dp, c], w_s.at[3], w_r.at[3], pair)
-
+    produce(0, 0, keys)
+
+    def step0(n, carry):
+        consume(0, n, vt)
+        produce(0, n + 1, keys)
+        give(0, n)
+        return carry
+
+    lax.fori_loop(0, 3, step0, 0)
+    consume(0, 3, vt)
+    give(0, 3)
+    wait(wcol.at[0, :, 0], w_r.at[0])
+    send(wcol.at[near, :, c], wcol.at[near, :, c], w_s.at[2], w_r.at[2], pair)
+
+    keys1, vt1 = keys_of(1)
     wait(enc, load_sem.at[3])
     wait(encb.at[0, pl.ds(0, 3), 0], enc_r.at[0])
     for d in (2, 1, 3):
         send(encb.at[y, :, c], encb.at[y, :, c], enc_s.at[1], enc_r.at[1], ypeer[d])
-
-    keys1, vt1 = keys_of(1)
-    for h in (0, 1):
-
-        def loop1(it, carry):
-            block(1, h, it, keys1, vt1)
-            return carry
-
-        lax.fori_loop(0, 2, loop1, 0)
-        if h == 0:
-            combine(0, 0)
-            combine(0, 1)
-            share(0, pl.ds(0, TOK), 0)
+    produce(1, 0, keys1)
+
+    def step1(n, carry):
+        consume(1, n, vt1)
+        produce(1, n + 1, keys1)
+        give(1, n)
+        return carry
+
+    lax.fori_loop(0, 3, step1, 0)
+    wait(wcol.at[0, 0, 0], w_r.at[1])
+    send(wcol.at[far, dp, c], wcol.at[far, dp, c], w_s.at[3], w_r.at[3], pair)
+    consume(1, 3, vt1)
+    give(1, 3)
+    combine(0, 0)
+    combine(0, 1)
+    share(0, pl.ds(0, TOK), 0)
     combine(1, 0)
     share(1, pl.ds(0, 64), 1)
+    combine(1, 1)
+    share(1, pl.ds(64, 64), 2)
 
     wait(wcol.at[0, :, 0], w_r.at[2])
     wait(wcol.at[0, 0, 0], w_r.at[3])
@@ -255,8 +292,6 @@
         send(wcol.at[s, :, c], wcol.at[s, :, c], w_s.at[4], w_r.at[4], mate)
     wait(encb.at[0:3, :, 0], enc_r.at[1])
     send(encb.at[:, :, c], encb.at[:, :, c], enc_s.at[2], enc_r.at[2], mate)
-    combine(1, 1)
-    share(1, pl.ds(64, 64), 2)
 
     def first_end(h):
         rows = pl.ds(64 * h, 64)
@@ -414,8 +449,10 @@
     d_out[...] = dacc[...].astype(BF)
 
     for j in (0, 1):
-        for n in (0, 1, 2):
-            wait(qkv.at[j, n, pl.ds(0, 7)], qkv_s.at[j, n])
+        wait(qkv.at[j, 0, pl.ds(0, 7)], qkv_s.at[j, 0])
+        for n in (0, 1):
+            wait(qkv.at[j, 0, pl.ds(0, 5)], qkv_s.at[j, 1 + n])
+            wait(qkv.at[j, 0, pl.ds(0, 2)], kv_s.at[j, n])
         for h in (0, 1):
             wait(osend.at[j, h, pl.ds(0, 7)], o_s.at[j, h])
     wait(wcol.at[0, :, 0], w_s.at[0])
@@ -498,6 +535,8 @@
             VMEM((4, 4, 2, 48, 384), BF),
             VMEM((2, 2, 8, 80, HD), BF),
             VMEM((2, 4, 2, 2, 80, HD), BF),
+            VMEM((2, 8 * TOK, 256), F32),
+            VMEM((2, 8, 256), F32),
             VMEM((TOK, 384), BF),
             VMEM((2, 4, 16, 384), BF),
             VMEM((4, 2, 2 * TOK, 256), BF),
@@ -533,6 +572,8 @@
             dma((5,)),
             dma((2, 3)),
             dma((2, 3)),
+            dma((2, 2)),
+            dma((2, 2)),
             dma((5,)),
             dma((5,)),
             dma((3,)),

time: 102 us -> 105 us (1.029)
  the two profiles are of different devices: /device:TPU:10 before, /device:TPU:19 now
where the time goes in v3:
time: 105 us
  Pallas kernels  104 us (99%)
  between operations  1.29 us (1%)
    pallas_call x1, Pallas kernels, local(): pl.pallas_call(kernel, name='alignment', out_shape=(jax.ShapeDtypeStruct(...  102 us

profile of v3, /device:TPU:19, one launch (start us, length us, event | category | flops | bytes accessed | tf_op | source)
XLA Modules:
  0.0 105.3 jit_solution(11190860004354316701)
XLA Ops:
  1.3 102.2 %alignment.1 = (bf16[128,512]{1,0:T(8,128)(2,1)}, f32[64,512]{1,0:T(8,128)}, f32[48,512]{1,0:T(8,128)}) custom-call(bf16[128,512]{1,0:T(8,128)(2,1)} %bitcast.16, bf16[128,512]{1,0:T(8,128)(2,1)} %bitcast.17, bf16[128,512]{1,0:T(8,128)(2,1)} %bitcast.18, bf16[128,512]{1,0:T(8,128)(2,1)} %bitcast.19, bf16[1000,512]{1,0:T(8,128)(2,1)} %gate_in.1, ...), custom_call_target="tpu_custom_call" | custom-call | flops 2500000000 | bytes 16000000 | tf_op jit(solution)/shard_map/alignment/pallas_call | solution.py:519
  103.5 1.8 %keep.1 = (bf16[128,512]{1,0:T(8,128)(2,1)}, f32[64,512]{1,0:T(8,128)}, f32[48,512]{1,0:T(8,128)}) custom-call(bf16[128,512]{1,0:T(8,128)(2,1)} %get-tuple-element.9.a, f32[64,512]{1,0:T(8,128)} %get-tuple-element.10.b, f32[48,512]{1,0:T(8,128)} %get-tuple-element.11.c), custom_call_target="tpu_custom_call" | custom-call | tf_op jit(solution)/shard_map/keep/pallas_call | solution.py:608

commit v4 on v3

--- a/solution.py
+++ b/solution.py
@@ -278,8 +278,9 @@
     consume(1, 3, vt1)
     give(1, 3)
     combine(0, 0)
+    share(0, pl.ds(0, 64), 0)
     combine(0, 1)
-    share(0, pl.ds(0, TOK), 0)
+    share(0, pl.ds(64, 64), 0)
     combine(1, 0)
     share(1, pl.ds(0, 64), 1)
     combine(1, 1)
@@ -327,10 +328,8 @@
         mrows = pl.ds(TOK + 64 * h, 64)
         wait(g2.at[0:48], g_r.at[h])
         send(g2.at[rows], g2.at[mrows], mate_s.at[2 + h], mate_r.at[2 + h], mate)
-        v = inner[rows]
-        sig = 1.0 / (1.0 + jnp.exp(-v))
         grad_act = dot(g2[rows], wout[...], 1, 1)
-        gi[t, rows] = (grad_act * (sig * (1.0 + v * (1.0 - sig)))).astype(BF)
+        gi[t, rows] = (grad_act * inner[rows]).astype(BF)
         for d in (2, 1, 3):
             send(gi.at[t, rows], gi.at[t, rows], gi_s, gi_r.at[d - 1], zpeer[d])
         send(gi.at[t, rows, other], gia.at[mrows], mate_s.at[4 + h], mate_r.at[4 + h], mate)
@@ -358,6 +357,9 @@
     send(hidf.at[:, :, pl.ds(0, TOK)], hidf.at[:, :, pl.ds(TOK, TOK)], mate_s.at[0], mate_r.at[0], mate)
     a2[0:TOK] = act[:, half]
     send(act.at[:, other], a2.at[pl.ds(TOK, TOK)], mate_s.at[1], mate_r.at[1], mate)
+    v = inner[...]
+    sig = 1.0 / (1.0 + jnp.exp(-v))
+    inner[...] = sig * (1.0 + v * (1.0 - sig))
     for h in (0, 1):
         loss(h)
     for h in (0, 1):

time: 105 us -> 101 us (0.962)
  the two profiles are of different devices: /device:TPU:19 before, /device:TPU:25 now
where the time goes in v4:
time: 101 us
  Pallas kernels  99.4 us (98%)
  between operations  1.29 us (1%)
    pallas_call x1, Pallas kernels, local(): pl.pallas_call(kernel, name='alignment', out_shape=(jax.ShapeDtypeStruct(...  97.7 us

profile of v4, /device:TPU:25, one launch (start us, length us, event | category | flops | bytes accessed | tf_op | source)
XLA Modules:
  0.0 100.7 jit_solution(5504777226535566261)
XLA Ops:
  1.3 97.7 %alignment.1 = (bf16[128,512]{1,0:T(8,128)(2,1)}, f32[64,512]{1,0:T(8,128)}, f32[48,512]{1,0:T(8,128)}) custom-call(bf16[128,512]{1,0:T(8,128)(2,1)} %bitcast.16, bf16[128,512]{1,0:T(8,128)(2,1)} %bitcast.17, bf16[128,512]{1,0:T(8,128)(2,1)} %bitcast.18, bf16[128,512]{1,0:T(8,128)(2,1)} %bitcast.19, bf16[1000,512]{1,0:T(8,128)(2,1)} %gate_in.1, ...), custom_call_target="tpu_custom_call" | custom-call | flops 2500000000 | bytes 16000000 | tf_op jit(solution)/shard_map/alignment/pallas_call | solution.py:521
  98.9 1.8 %keep.1 = (bf16[128,512]{1,0:T(8,128)(2,1)}, f32[64,512]{1,0:T(8,128)}, f32[48,512]{1,0:T(8,128)}) custom-call(bf16[128,512]{1,0:T(8,128)(2,1)} %get-tuple-element.9.a, f32[64,512]{1,0:T(8,128)} %get-tuple-element.10.b, f32[48,512]{1,0:T(8,128)} %get-tuple-element.11.c), custom_call_target="tpu_custom_call" | custom-call | tf_op jit(solution)/shard_map/keep/pallas_call | solution.py:610
